TPU v7x, 32 devices: a whole 2x2x4 slice. The times are simulated.
32 devices in a mesh: tile: 8 (over y, x, core), wave: 4 (over z).
Axes of the slice: x: 2, y: 2, z: 4, core: 2. Of those that a mesh axis runs over, the one named last changes fastest.
Arguments:
- maps: float32 [4, 128, 1024], P(None, None, 'tile'), may hold values from 0 to 2
- measured: float32 [16, 128, 128], P('tile'), may hold values from 0 to 8
- offsets: int32 [16], P('tile'), may hold values from -64 to 64, as said below
- probe: float32 [48, 2, 128, 128], P('wave'), may hold values from -6 to 6
- spectrum: float32 [48], P('wave'), may hold values from 0.05 to 0.5
- wave_index: int32 [48], P('wave'), may hold values from 0 to 47, each once
- edge_band: int32 [48, 4], P('wave'), may hold values from 0 to 2
- band_coef: float32 [2, 3, 4], replicated, may hold values from 0.1 to 0.8
Outputs:
- new_maps: float32 [4, 128, 1024], P(None, None, 'tile')
Inputs may be any that keep to these rules, and one draw needn't show every extreme that they name: `offsets`: a frame reaches at most 64 columns into either neighbouring tile; in every tile one frame starts exactly 64 columns before the tile and another ends exactly 64 columns after it. `wave_index`: each wavelength is held by exactly one slot.
All inputs are finite; a program needn't handle non-finite values.
Results may differ from a plain program's by a relative error of at most 0.0024.
Values sent between devices are 32-bit elements; how exact they have to be, the bound alone decides.
No kernel may reach another device: no remote copies, remote signals or barrier semaphores. Data moves between devices by JAX's collectives and lax.ppermute only.
A program may use at most 64 MiB of HBM per device.

v0:
```python
import math
import jax
import jax.numpy as jnp
from jax import lax
from jax.sharding import PartitionSpec as P

WAVES = 48
relax = 4.0
floor_level = 1.0


def padded(block, sides, width):
    for axis, dim in sides:
        count = lax.axis_size(axis)
        forward = [(i, i + 1) for i in range(count - 1)]
        backward = [(target, source) for source, target in forward]
        low = lax.ppermute(
            lax.slice_in_dim(block, block.shape[dim] - width, None, axis=dim), axis, forward
        )
        high = lax.ppermute(lax.slice_in_dim(block, 0, width, axis=dim), axis, backward)
        block = jnp.concatenate([low, block, high], axis=dim)
    return block


def chirp_table(which_wave, length):
    centred = jnp.arange(length, dtype=jnp.int32) - length // 2
    product = (centred[:, None] * centred[None, :]).astype(jnp.float32)
    sampling = 0.6 + 0.4 * which_wave.astype(jnp.float32) / (WAVES - 1)
    phase_angle = -2.0 * math.pi / length * sampling[..., None, None] * product
    normaliser = 1.0 / math.sqrt(length)
    return (
        (jnp.cos(phase_angle) * normaliser).astype(jnp.bfloat16),
        (jnp.sin(phase_angle) * normaliser).astype(jnp.bfloat16),
    )


def left_product(table, data):
    return jnp.einsum("kn,fnj->fkj", table, data, preferred_element_type=jnp.float32)


def right_product(data, table):
    return jnp.einsum("fkn,nj->fkj", data, table, preferred_element_type=jnp.float32)


def transform(table_re, table_im, data_re, data_im):
    mid_re = (left_product(table_re, data_re) - left_product(table_im, data_im)).astype(
        jnp.bfloat16
    )
    mid_im = (left_product(table_re, data_im) + left_product(table_im, data_re)).astype(
        jnp.bfloat16
    )
    out_re = right_product(mid_re, table_re) - right_product(mid_im, table_im)
    out_im = right_product(mid_re, table_im) + right_product(mid_im, table_re)
    return (out_re, out_im)


def fold_rims(interior, arrived, margin):
    columns = interior.shape[2]
    left_part = interior[:, :, :margin] + arrived[:, :, :margin]
    middle = interior[:, :, margin : columns - margin]
    right_part = interior[:, :, columns - margin :] + arrived[:, :, arrived.shape[2] - margin :]
    return jnp.concatenate([left_part, middle, right_part], axis=2)


def edge_cells(accumulated, margin):
    width = accumulated.shape[2]
    return jnp.concatenate(
        [accumulated[:, :, :margin], accumulated[:, :, width - margin :]], axis=2
    )


def place_frames(stacked, offsets, columns, margin):
    frame_count, channels, length = (stacked.shape[0], stacked.shape[1], stacked.shape[2])
    accumulated = jnp.zeros((channels, length, columns + 2 * margin), jnp.float32)
    for frame in range(frame_count):
        current = lax.dynamic_slice_in_dim(accumulated, offsets[frame] + margin, length, 2)
        accumulated = lax.dynamic_update_slice_in_dim(
            accumulated, current + stacked[frame], offsets[frame] + margin, 2
        )
    return accumulated


def per_device(maps, measured, offsets, probe, spectrum, wave_index, edge_band, band_coef):
    materials, length, columns = maps.shape
    frame_count = measured.shape[0]
    band_count = band_coef.shape[1]
    margin = length // 2
    extended = padded(maps, (("tile", 2),), margin)
    windows = jnp.stack(
        [
            lax.dynamic_slice_in_dim(extended, offsets[frame] + margin, length, 2)
            for frame in range(frame_count)
        ]
    )
    onehot = (edge_band[:, :, None] == jnp.arange(band_count, dtype=jnp.int32)).astype(jnp.float32)
    coefficient = jnp.einsum("smb,cbm->csm", onehot, band_coef, precision=lax.Precision.HIGHEST)

    def forward_slot(partial_value, inputs):
        wave_probe, absorb_coef, phase_coef, weight, which_wave = inputs
        absorb = jnp.einsum("m,fmrk->frk", absorb_coef, windows, precision=lax.Precision.HIGHEST)
        phase_sum = jnp.einsum("m,fmrk->frk", phase_coef, windows, precision=lax.Precision.HIGHEST)
        damping = jnp.exp(-absorb)
        obj_re = damping * jnp.cos(phase_sum)
        obj_im = damping * jnp.sin(phase_sum)
        psi_re = wave_probe[0] * obj_re - wave_probe[1] * obj_im
        psi_im = wave_probe[0] * obj_im + wave_probe[1] * obj_re
        table_re, table_im = chirp_table(which_wave, length)
        far_re, far_im = transform(
            table_re, table_im, psi_re.astype(jnp.bfloat16), psi_im.astype(jnp.bfloat16)
        )
        partial_value = partial_value + weight * (far_re * far_re + far_im * far_im)
        return (partial_value, (table_re, table_im, psi_re, psi_im, far_re, far_im))

    partial_value = jnp.zeros((frame_count, length, length), jnp.float32)
    partial_value, stored = lax.scan(
        forward_slot, partial_value, (probe, coefficient[0], coefficient[1], spectrum, wave_index)
    )
    intensity = lax.psum(partial_value, "wave")
    shortfall = jnp.sqrt(measured / jnp.maximum(intensity, floor_level)) - 1.0

    def backward_slot(totals, inputs):
        absorb_coef, phase_coef, weight, table_re, table_im, psi_re, psi_im, far_re, far_im = inputs
        factor = weight * shortfall
        back_re, back_im = transform(
            table_re,
            -table_im,
            (factor * far_re).astype(jnp.bfloat16),
            (factor * far_im).astype(jnp.bfloat16),
        )
        cross_re = psi_re * back_re + psi_im * back_im
        cross_im = psi_re * back_im - psi_im * back_re
        gradient = (
            cross_re[:, None] * (-absorb_coef)[None, :, None, None]
            + cross_im[:, None] * phase_coef[None, :, None, None]
        )
        power_sum = weight * (psi_re * psi_re + psi_im * psi_im)
        return ((totals[0] + gradient, totals[1] + power_sum), None)

    start_totals = (
        jnp.zeros((frame_count, materials, length, length), jnp.float32),
        jnp.zeros((frame_count, length, length), jnp.float32),
    )
    table_re, table_im, psi_re, psi_im, far_re, far_im = stored
    (gradient, power_sum), _ = lax.scan(
        backward_slot,
        start_totals,
        (
            coefficient[0],
            coefficient[1],
            spectrum,
            table_re,
            table_im,
            psi_re,
            psi_im,
            far_re,
            far_im,
        ),
    )
    stacked = jnp.concatenate([gradient, power_sum[:, None]], axis=1)
    accumulated = place_frames(stacked, offsets, columns, margin)
    arrived = padded(edge_cells(accumulated, margin), (("tile", 2),), margin)
    summed = lax.psum(
        fold_rims(accumulated[:, :, margin : margin + columns], arrived, margin), "wave"
    )
    return maps + relax * summed[:materials] / (summed[materials] + 1.0)


def solution(mesh):
    in_specs = (
        P(None, None, "tile"),
        P("tile", None, None),
        P("tile"),
        P("wave", None, None, None),
        P("wave"),
        P("wave"),
        P("wave", None),
        P(),
    )
    out_specs = P(None, None, "tile")
    return jax.shard_map(
        per_device, mesh=mesh, in_specs=in_specs, out_specs=out_specs, check_vma=False
    )
```

profile of v0, /device:TPU:0, one launch (start us, length us, event | category | flops | bytes accessed | tf_op | source)
XLA Modules:
  0.0 355.2 jit_solution(11261539689890777825)
XLA Ops:
  7.7 2.4 collective-permute-start
  10.1 1.3 collective-permute-start.1
  11.4 1.4 fusion.117
  18.9 154.0 %while.38 = (s32[]{:T(128)}, f32[2,128,128]{2,1,0:T(8,128)S(1)}, bf16[12,128,128]{2,1,0:T(8,128)(2,1)S(1)}, bf16[12,128,128]{2,1,0:T(8,128)(2,1)S(1)}, f32[12,2,...) while((s32[]{:T(128)}, f32[2,128,128]{2,1,0:T(8,128)S(1)}, ...), condition=%wide.region_1.2_spmd.clone, body=%wide.region_0.1_spmd.clone.sunk | while | flops 71778440 | bytes 5973319 | solution.py:115
  18.9 1.3 fusion.204
  20.2 1.3 fusion.205
  31.7 1.3 fusion.204
  33.0 1.3 fusion.205
  44.5 1.3 fusion.204
  45.9 1.3 fusion.205
  57.3 1.3 fusion.204
  58.7 1.3 fusion.205
  70.2 1.3 fusion.204
  71.5 1.3 fusion.205
  83.0 1.3 fusion.204
  84.4 1.3 fusion.205
  95.8 1.3 fusion.204
  97.2 1.3 fusion.205
  99.7 1.3 bitcast_dynamic-update-slice_fusion.7
  108.7 1.3 fusion.204
  110.1 1.3 fusion.205
  122.9 1.3 fusion.205
  134.3 1.3 fusion.204
  135.7 1.3 fusion.205
  148.6 1.3 fusion.205
  160.0 1.3 fusion.204
  161.4 1.3 fusion.205
  173.6 39.1 %all-reduce.3.cloned.1.call-done = f32[2,128,128]{2,1,0:T(8,128)} async-done(((f32[2,128,128]{2,1,0:T(8,128)}), f32[2,128,128]{2,1,0:T(8,128)}) %all-reduce.3.cloned.1.call-update) | async-done | bytes 131088 | tf_op jit(solution)/shard_map/psum | solution.py:118
  213.7 70.5 %while.39 = (s32[]{:T(128)}, f32[2,4,128,128]{3,2,1,0:T(8,128)S(1)}, f32[2,128,128]{2,1,0:T(8,128)S(1)}, f32[12,2,128,128]{2,3,1,0:T(8,128)}, f32[12]{0:T(128)S(...) while((s32[]{:T(128)}, ...), condition=%wide.region_4.5_spmd.clone, body=%wide.region_3.4_spmd.clone.sunk | while | flops 68583424 | bytes 5898552 | solution.py:144
  214.3 1.6 fusion.229
  220.2 1.6 fusion.229
  226.1 1.6 fusion.229
  232.0 1.6 fusion.229
  237.8 1.6 fusion.229
  243.7 1.6 fusion.229
  249.6 1.6 fusion.229
  255.5 1.6 fusion.229
  261.4 1.6 fusion.229
  267.2 1.6 fusion.229
  273.1 1.6 fusion.229
  279.0 1.6 fusion.229
  284.4 3.1 dynamic_update_slice.44
  287.6 4.5 %dynamic_update_slice.45 = f32[5,128,256]{2,1,0:T(8,128)S(1)} dynamic-update-slice(f32[5,128,256]{2,1,0:T(8,128)S(1)} %dynamic_update_slice.44, f32[5,128,128]{2,1,0:T(8,128)S(1)} %fusion.110, s32[]{:T(128)} %constant.93.clone.1, s32[]{:T(128)} %constant.93.clone.1, s32[]{:T(128)S(6)} %select_n.10) | dynamic-update-slice | bytes 655364 | tf_op jit(solution)/shard_map/dynamic_update_slice | solution.py:77
  292.3 1.3 collective-permute-start.2
  295.0 1.4 collective-permute-start.3
  296.5 6.6 %collective-permute-done.3 = f32[5,128,64]{2,1,0:T(8,128)S(1)} collective-permute-done((f32[5,128,64]{2,1,0:T(8,128)S(1)}, f32[5,128,64]{2,1,0:T(8,128)S(1)}, u32[]{:S(2)}, u32[]{:S(2)}) %collective-permute-start.3) | collective-permute-done | bytes 163872 | tf_op jit(solution)/shard_map/ppermute | solution.py:20
  304.0 41.8 %all-reduce.5.cloned.1.call-done = f32[5,128,128]{2,1,0:T(8,128)} async-done(((f32[5,128,128]{2,1,0:T(8,128)}), f32[5,128,128]{2,1,0:T(8,128)}) %all-reduce.5.cloned.1.call-update) | async-done | bytes 327696 | tf_op jit(solution)/shard_map/psum | solution.py:162
  346.7 1.7 fusion.112
  (441 shorter events, 175.4 us)
Async XLA Ops:
  6.5 206.2 %all-reduce.3.cloned.1.call-start = ((), (), s32[]{:S(2)}) async-start(), calls=%async_computation | async-start | bytes 262144 | tf_op jit(solution)/shard_map/psum | solution.py:118
  7.7 9.6 %collective-permute-start = (f32[4,128,64]{2,1,0:T(8,128)S(1)}, f32[4,128,64]{2,1,0:T(8,128)S(1)}, u32[]{:S(2)}, u32[]{:S(2)}) collective-permute-start(f32[4,128,64]{2,1,0:T(8,128)S(1)} %get-tuple-element.457), channel_id=1, source_target_pairs={{0,4},{4,8},{8,12},{12,16},{16,20},{20,24},{24,28},{1,5},{5,9},{9,... | collective-permute-start | bytes 393224 | tf_op jit(solution)/shard_map/ppermute | solution.py:17
  10.1 7.3 %collective-permute-start.1 = (f32[4,128,64]{2,1,0:T(8,128)S(1)}, f32[4,128,64]{2,1,0:T(8,128)S(1)}, u32[]{:S(2)}, u32[]{:S(2)}) collective-permute-start(f32[4,128,64]{2,1,0:T(8,128)S(1)} %get-tuple-element.458), channel_id=1, source_target_pairs={{4,0},{8,4},{12,8},{16,12},{20,16},{24,20},{28,24},{5,1},{9,5},{13... | collective-permute-start | bytes 393224 | tf_op jit(solution)/shard_map/ppermute | solution.py:20
  17.3 1.5 copy-start.3
  17.3 1.5 copy-start.4
  18.9 193.9 %copy-start.2 = (f32[2,128,128]{2,1,0:T(8,128)S(1)}, f32[2,128,128]{2,1,0:T(8,128)}, u32[]{:S(2)}) copy-start(f32[2,128,128]{2,1,0:T(8,128)} %param.13) | copy-start | bytes 393220
  172.9 0.7 copy-start
  173.6 172.3 %all-reduce.5.cloned.1.call-start = ((), (), s32[]{:S(2)}) async-start(), calls=%async_computation.1 | async-start | bytes 655360 | tf_op jit(solution)/shard_map/psum | solution.py:162
  292.3 2.5 collective-permute-start.2
  295.0 51.7 %copy-start.1 = (f32[4,128,128]{2,1,0:T(8,128)S(1)}, f32[4,128,128]{2,1,0:T(8,128)}, u32[]{:S(2)}) copy-start(f32[4,128,128]{2,1,0:T(8,128)} %param.12) | copy-start | bytes 786436
  295.0 8.1 %collective-permute-start.3 = (f32[5,128,64]{2,1,0:T(8,128)S(1)}, f32[5,128,64]{2,1,0:T(8,128)S(1)}, u32[]{:S(2)}, u32[]{:S(2)}) collective-permute-start(f32[5,128,64]{2,1,0:T(8,128)S(1)} %get-tuple-element.454), channel_id=1, source_target_pairs={{4,0},{8,4},{12,8},{16,12},{20,16},{24,20},{28,24},{5,1},{9,5},{13... | collective-permute-start | bytes 491528 | tf_op jit(solution)/shard_map/ppermute | solution.py:20
Sparse Core Ops, SparseCore 0:
  173.7 39.0 all-reduce.2
  304.2 41.6 all-reduce.4
where the time goes:
time: 357 us; the launch traced here: 355 us
  matrix products  114 us (32%)
  waiting for transfers between devices  88.8 us (25%)
  local copies, waits for them, and re-layouts  72.2 us (20%)
  other arithmetic  46.8 us (13%)
  between operations  16.3 us (5%)
  loops' own time  10.2 us (3%)
  starting transfers between devices  6.44 us (2%)
    dot_general x96, matrix products, right_product(): jnp.einsum('fkn,nj->fkj', data, table, preferred_element_type=jnp.float32)  53.6 us
    psum x1, waiting for transfers between devices, per_device(): lax.psum(fold_rims(accumulated[:, :, margin:margin + columns], arrived, m...  41.8 us
    psum x1, waiting for transfers between devices, per_device(): intensity = lax.psum(partial_value, 'wave')  39.1 us
    dynamic_slice x72, local copies, waits for them, and re-layouts, per_device(): lax.scan(forward_slot, partial_value, (probe, coefficient[0], coefficient...  36.9 us
    dot_general x96, matrix products, left_product(): jnp.einsum('kn,fnj->fkj', table, data, preferred_element_type=jnp.float32)  29.9 us
    convert_element_type x12, other arithmetic, backward_slot(): (factor * far_im).astype(jnp.bfloat16)  19.7 us
    dynamic_update_slice x24, other arithmetic, per_device(): lax.scan(forward_slot, partial_value, (probe, coefficient[0], coefficient...  19 us
    dot_general x12, matrix products, forward_slot(): jnp.einsum('m,fmrk->frk', absorb_coef, windows, precision=lax.Precision.H...  15 us
  transfers between devices with their start and end apart: 6, of which 4 were waited for; matrix products, arithmetic and copies ran while one was open for 1% of the time, Pallas kernels for 0%

commit v1 on v0

--- a/solution.py
+++ b/solution.py
@@ -159,9 +159,8 @@
     stacked = jnp.concatenate([gradient, power_sum[:, None]], axis=1)
     accumulated = place_frames(stacked, offsets, columns, margin)
     arrived = padded(edge_cells(accumulated, margin), (("tile", 2),), margin)
-    summed = lax.psum(
-        fold_rims(accumulated[:, :, margin : margin + columns], arrived, margin), "wave"
-    )
+    get_kinds = lambda here_x: jnp.sum(lax.all_gather(here_x, axis_name="wave"), axis=0)
+    summed = get_kinds(fold_rims(accumulated[:, :, margin : margin + columns], arrived, margin))
     return maps + relax * summed[:materials] / (summed[materials] + 1.0)
 
 

time: 357 us -> 353 us (0.989)
    psum x1 -> x0, waiting for transfers between devices: 41.8 us -> none  [per_device(): lax.psum(fold_rims(accumulated[:, :, margin:margin + columns], arrived, m...]
    all_gather x0 -> x1, waiting for transfers between devices: none -> 38.3 us  [per_device(): lax.all_gather(here_x, axis_name='wave')]
where the time goes in v1:
time: 353 us; the launch traced here: 351 us
  matrix products  114 us (32%)
  waiting for transfers between devices  85.3 us (24%)
  local copies, waits for them, and re-layouts  72.2 us (20%)
  other arithmetic  46.4 us (13%)
  between operations  16.4 us (5%)
  loops' own time  10.2 us (3%)
  starting transfers between devices  6.31 us (2%)
    dot_general x96, matrix products, right_product(): jnp.einsum('fkn,nj->fkj', data, table, preferred_element_type=jnp.float32)  53.6 us
    psum x1, waiting for transfers between devices, per_device(): intensity = lax.psum(partial_value, 'wave')  39.1 us
    all_gather x1, waiting for transfers between devices, per_device(): lax.all_gather(here_x, axis_name='wave')  38.3 us
    dynamic_slice x72, local copies, waits for them, and re-layouts, per_device(): lax.scan(forward_slot, partial_value, (probe, coefficient[0], coefficient...  36.9 us
    dot_general x96, matrix products, left_product(): jnp.einsum('kn,fnj->fkj', table, data, preferred_element_type=jnp.float32)  29.9 us
    convert_element_type x12, other arithmetic, backward_slot(): (factor * far_im).astype(jnp.bfloat16)  19.7 us
    dynamic_update_slice x24, other arithmetic, per_device(): lax.scan(forward_slot, partial_value, (probe, coefficient[0], coefficient...  19 us
    dot_general x12, matrix products, forward_slot(): jnp.einsum('m,fmrk->frk', absorb_coef, windows, precision=lax.Precision.H...  15 us
  transfers between devices with their start and end apart: 6, of which 4 were waited for; matrix products, arithmetic and copies ran while one was open for 1% of the time, Pallas kernels for 0%

profile of v1, /device:TPU:0, one launch (start us, length us, event | category | flops | bytes accessed | tf_op | source)
XLA Modules:
  0.0 351.2 jit_solution(1813766870148725541)
XLA Ops:
  7.7 2.4 collective-permute-start
  10.1 1.3 collective-permute-start.1
  11.4 1.4 fusion.117
  18.9 154.0 %while.38 = (s32[]{:T(128)}, f32[2,128,128]{2,1,0:T(8,128)S(1)}, bf16[12,128,128]{2,1,0:T(8,128)(2,1)S(1)}, bf16[12,128,128]{2,1,0:T(8,128)(2,1)S(1)}, f32[12,2,...) while((s32[]{:T(128)}, f32[2,128,128]{2,1,0:T(8,128)S(1)}, ...), condition=%wide.region_1.2_spmd.clone, body=%wide.region_0.1_spmd.clone.sunk | while | flops 71778440 | bytes 5973319 | solution.py:115
  18.9 1.3 fusion.204
  20.2 1.3 fusion.205
  31.7 1.3 fusion.204
  33.0 1.3 fusion.205
  44.5 1.3 fusion.204
  45.9 1.3 fusion.205
  57.3 1.3 fusion.204
  58.7 1.3 fusion.205
  70.2 1.3 fusion.204
  71.5 1.3 fusion.205
  83.0 1.3 fusion.204
  84.4 1.3 fusion.205
  95.8 1.3 fusion.204
  97.2 1.3 fusion.205
  99.7 1.3 bitcast_dynamic-update-slice_fusion.7
  108.7 1.3 fusion.204
  110.1 1.3 fusion.205
  122.9 1.3 fusion.205
  134.3 1.3 fusion.204
  135.7 1.3 fusion.205
  148.6 1.3 fusion.205
  160.0 1.3 fusion.204
  161.4 1.3 fusion.205
  173.6 39.1 %all-reduce.2.cloned.1.call-done = f32[2,128,128]{2,1,0:T(8,128)} async-done(((f32[2,128,128]{2,1,0:T(8,128)}), f32[2,128,128]{2,1,0:T(8,128)}) %all-reduce.2.cloned.1.call-update) | async-done | bytes 131088 | tf_op jit(solution)/shard_map/psum | solution.py:118
  213.7 70.5 %while.39 = (s32[]{:T(128)}, f32[2,4,128,128]{3,2,1,0:T(8,128)S(1)}, f32[2,128,128]{2,1,0:T(8,128)S(1)}, f32[12,2,128,128]{2,3,1,0:T(8,128)}, f32[12]{0:T(128)S(...) while((s32[]{:T(128)}, ...), condition=%wide.region_4.5_spmd.clone, body=%wide.region_3.4_spmd.clone.sunk | while | flops 68583424 | bytes 5898552 | solution.py:144
  214.3 1.6 fusion.229
  220.2 1.6 fusion.229
  226.1 1.6 fusion.229
  232.0 1.6 fusion.229
  237.8 1.6 fusion.229
  243.7 1.6 fusion.229
  249.6 1.6 fusion.229
  255.5 1.6 fusion.229
  261.4 1.6 fusion.229
  267.2 1.6 fusion.229
  273.1 1.6 fusion.229
  279.0 1.6 fusion.229
  284.4 3.1 dynamic_update_slice.44
  287.6 4.5 %dynamic_update_slice.45 = f32[5,128,256]{2,1,0:T(8,128)S(1)} dynamic-update-slice(f32[5,128,256]{2,1,0:T(8,128)S(1)} %dynamic_update_slice.44, f32[5,128,128]{2,1,0:T(8,128)S(1)} %fusion.110, s32[]{:T(128)} %constant.94.clone.1, s32[]{:T(128)} %constant.94.clone.1, s32[]{:T(128)S(6)} %select_n.10) | dynamic-update-slice | bytes 655364 | tf_op jit(solution)/shard_map/dynamic_update_slice | solution.py:77
  292.3 1.3 collective-permute-start.2
  295.0 1.3 collective-permute-start.3
  296.3 6.6 %collective-permute-done.3 = f32[5,128,64]{2,1,0:T(8,128)S(1)} collective-permute-done((f32[5,128,64]{2,1,0:T(8,128)S(1)}, f32[5,128,64]{2,1,0:T(8,128)S(1)}, u32[]{:S(2)}, u32[]{:S(2)}) %collective-permute-start.3) | collective-permute-done | bytes 163872 | tf_op jit(solution)/shard_map/ppermute | solution.py:20
  303.9 38.3 %all-gather.3.cloned.1.call-done = f32[20,128,128]{2,1,0:T(8,128)} async-done(((f32[5,128,128]{2,1,0:T(8,128)}), f32[20,128,128]{2,1,0:T(8,128)}) %all-gather.3.cloned.1.call-update) | async-done | bytes 1310736 | tf_op jit(solution)/shard_map/all_gather | solution.py:162
  342.2 1.4 reduce_sum.9
  (442 shorter events, 175.3 us)
Async XLA Ops:
  6.5 206.2 %all-reduce.2.cloned.1.call-start = ((), (), s32[]{:S(2)}) async-start(), calls=%async_computation | async-start | bytes 262144 | tf_op jit(solution)/shard_map/psum | solution.py:118
  7.7 9.6 %collective-permute-start = (f32[4,128,64]{2,1,0:T(8,128)S(1)}, f32[4,128,64]{2,1,0:T(8,128)S(1)}, u32[]{:S(2)}, u32[]{:S(2)}) collective-permute-start(f32[4,128,64]{2,1,0:T(8,128)S(1)} %get-tuple-element.484), channel_id=1, source_target_pairs={{0,4},{4,8},{8,12},{12,16},{16,20},{20,24},{24,28},{1,5},{5,9},{9,... | collective-permute-start | bytes 393224 | tf_op jit(solution)/shard_map/ppermute | solution.py:17
  10.1 7.3 %collective-permute-start.1 = (f32[4,128,64]{2,1,0:T(8,128)S(1)}, f32[4,128,64]{2,1,0:T(8,128)S(1)}, u32[]{:S(2)}, u32[]{:S(2)}) collective-permute-start(f32[4,128,64]{2,1,0:T(8,128)S(1)} %get-tuple-element.485), channel_id=1, source_target_pairs={{4,0},{8,4},{12,8},{16,12},{20,16},{24,20},{28,24},{5,1},{9,5},{13... | collective-permute-start | bytes 393224 | tf_op jit(solution)/shard_map/ppermute | solution.py:20
  17.3 1.5 copy-start.3
  17.3 1.5 copy-start.4
  18.9 193.9 %copy-start.2 = (f32[2,128,128]{2,1,0:T(8,128)S(1)}, f32[2,128,128]{2,1,0:T(8,128)}, u32[]{:S(2)}) copy-start(f32[2,128,128]{2,1,0:T(8,128)} %param.13) | copy-start | bytes 393220
  172.9 0.7 copy-start
  173.6 168.7 %all-gather.3.cloned.1.call-start = ((), (), s32[]{:S(2)}) async-start(), calls=%async_computation.1 | async-start | bytes 1638400 | tf_op jit(solution)/shard_map/all_gather | solution.py:162
  292.3 2.5 collective-permute-start.2
  295.0 7.9 %collective-permute-start.3 = (f32[5,128,64]{2,1,0:T(8,128)S(1)}, f32[5,128,64]{2,1,0:T(8,128)S(1)}, u32[]{:S(2)}, u32[]{:S(2)}) collective-permute-start(f32[5,128,64]{2,1,0:T(8,128)S(1)} %get-tuple-element.481), channel_id=1, source_target_pairs={{4,0},{8,4},{12,8},{16,12},{20,16},{24,20},{28,24},{5,1},{9,5},{13... | collective-permute-start | bytes 491528 | tf_op jit(solution)/shard_map/ppermute | solution.py:20
  303.0 40.7 %copy-start.1 = (f32[4,128,128]{2,1,0:T(8,128)S(1)}, f32[4,128,128]{2,1,0:T(8,128)}, u32[]{:S(2)}) copy-start(f32[4,128,128]{2,1,0:T(8,128)} %param.12) | copy-start | bytes 786436
Sparse Core Ops, SparseCore 0:
  173.7 39.0 all-reduce.1
  304.0 38.1 all-gather.2
